TPU v7x, 32 devices: a whole 2x2x4 slice. The times are simulated.
32 devices in a mesh: dp: 4 (over y, core), fsdp: 8 (over z, x).
Axes of the slice: x: 2, y: 2, z: 4, core: 2. Of those that a mesh axis runs over, the one named last changes fastest.
Arguments:
- frames: bfloat16 [16384, 768], P(('dp', 'fsdp')), may hold values from -6 to 6
- lengths: int32 [32, 2], P(('dp', 'fsdp')), may hold values from 0 to 512, as said below
- query_weight: bfloat16 [768, 768], P(('dp', 'fsdp')), may hold values from -0.21875 to 0.21875
- query_bias: bfloat16 [768], P(('dp', 'fsdp')), may hold values from -3 to 3
- key_weight: bfloat16 [768, 768], P(('dp', 'fsdp')), may hold values from -0.21875 to 0.21875
- value_weight: bfloat16 [768, 768], P(('dp', 'fsdp')), may hold values from -0.21875 to 0.21875
- value_bias: bfloat16 [768], P(('dp', 'fsdp')), may hold values from -3 to 3
- output_weight: bfloat16 [768, 768], P(('dp', 'fsdp')), may hold values from -2.5 to 2.5
- output_bias: bfloat16 [768], P(('dp', 'fsdp')), may hold values from -3 to 3
- first_gain: bfloat16 [768], P(('dp', 'fsdp')), may hold values from 0.5 to 1.5
- first_shift: bfloat16 [768], P(('dp', 'fsdp')), may hold values from -3 to 3
- inner_weight: bfloat16 [768, 3072], P(('dp', 'fsdp')), may hold values from -0.21875 to 0.21875
- inner_bias: bfloat16 [3072], P(('dp', 'fsdp')), may hold values from -3 to 3
- outer_weight: bfloat16 [3072, 768], P(('dp', 'fsdp')), may hold values from -0.109375 to 0.109375
- outer_bias: bfloat16 [768], P(('dp', 'fsdp')), may hold values from -3 to 3
- second_gain: bfloat16 [768], P(('dp', 'fsdp')), may hold values from 0.5 to 1.5
- second_shift: bfloat16 [768], P(('dp', 'fsdp')), may hold values from -3 to 3
- grad_out: bfloat16 [16384, 768], P(('dp', 'fsdp')), may hold values from -6 to 6
Outputs:
- layer_out: bfloat16 [16384, 768], P(('dp', 'fsdp'))
- frames_grad: bfloat16 [16384, 768], P(('dp', 'fsdp'))
- query_weight_grad: float32 [768, 768], P(('dp', 'fsdp'))
- query_bias_grad: float32 [768], P(('dp', 'fsdp'))
- key_weight_grad: float32 [768, 768], P(('dp', 'fsdp'))
- value_weight_grad: float32 [768, 768], P(('dp', 'fsdp'))
- value_bias_grad: float32 [768], P(('dp', 'fsdp'))
- output_weight_grad: float32 [768, 768], P(('dp', 'fsdp'))
- output_bias_grad: float32 [768], P(('dp', 'fsdp'))
- first_gain_grad: float32 [768], P(('dp', 'fsdp'))
- first_shift_grad: float32 [768], P(('dp', 'fsdp'))
- inner_weight_grad: float32 [768, 3072], P(('dp', 'fsdp'))
- inner_bias_grad: float32 [3072], P(('dp', 'fsdp'))
- outer_weight_grad: float32 [3072, 768], P(('dp', 'fsdp'))
- outer_bias_grad: float32 [768], P(('dp', 'fsdp'))
- second_gain_grad: float32 [768], P(('dp', 'fsdp'))
- second_shift_grad: float32 [768], P(('dp', 'fsdp'))
Inputs may be any that keep to these rules, and one draw needn't show every extreme that they name: `lengths`: row b holds block b's two utterances: slot 0 has 100 to 512 frames, slot 1 has 0 (empty) up to 512 minus slot 0; the block's remaining slots are padding. In one block, drawn from the seed, slot 0 fills all 512 slots.
All inputs are finite; a program needn't handle non-finite values.
Results may differ from a plain program's by a relative error of at most 0.015.
Values may be sent and summed in bfloat16 or wider, within the bound.
A program may use at most 192 MiB of HBM per device.

v0:
```python
import jax
import jax.numpy as jnp
from jax import lax
from jax.sharding import PartitionSpec as P

HEADS = 12


def layer_norm(values, gain_vec, shift_vec):
    center = values - jnp.mean(values, axis=-1, keepdims=True)
    spread = jnp.mean(center * center, axis=-1, keepdims=True)
    return center * lax.rsqrt(spread + 1e-05) * gain_vec + shift_vec


def exact_gelu(values):
    return jax.nn.gelu(values, approximate=False)


def matmul(left_side, right_side):
    return jnp.dot(left_side, right_side, preferred_element_type=jnp.float32)


def matmul_tn(left_side, right_side):
    return lax.dot_general(
        left_side, right_side, (((0,), (0,)), ((), ())), preferred_element_type=jnp.float32
    )


def matmul_nt(left_side, right_side):
    return lax.dot_general(
        left_side, right_side, (((1,), (1,)), ((), ())), preferred_element_type=jnp.float32
    )


def column_sums(values):
    return jnp.sum(values.astype(jnp.float32), axis=0)


def block_scores(query_block, key_heads, group_block, groups, score_scale):
    raw_scores = (
        jnp.einsum("qhd,khd->hqk", query_block, key_heads, preferred_element_type=jnp.float32)
        * score_scale
    )
    allowed = group_block[:, None] == groups[None, :]
    return jnp.where(allowed[None], raw_scores, -1e30)


def per_device(
    frames,
    lengths,
    query_weight,
    query_bias,
    key_weight,
    value_weight,
    value_bias,
    output_weight,
    output_bias,
    first_gain,
    first_shift,
    inner_weight,
    inner_bias,
    outer_weight,
    outer_bias,
    second_gain,
    second_shift,
    grad_out,
):
    frame_count = frames.shape[0]
    model_width = frames.shape[1]
    head_size = model_width // HEADS
    score_scale = head_size ** (-0.5)
    places = jnp.arange(frame_count, dtype=jnp.int32)
    bounds = jnp.stack([lengths[0, 0], lengths[0, 0] + lengths[0, 1]])
    groups = jnp.sum((places[:, None] >= bounds[None, :]).astype(jnp.int32), axis=1)
    live_mask = (places < bounds[-1]).astype(jnp.float32)
    gathered = (
        lax.all_gather(query_weight, ("dp", "fsdp"), axis=0, tiled=True),
        lax.all_gather(query_bias, ("dp", "fsdp"), axis=0, tiled=True),
        lax.all_gather(key_weight, ("dp", "fsdp"), axis=0, tiled=True),
        lax.all_gather(value_weight, ("dp", "fsdp"), axis=0, tiled=True),
        lax.all_gather(value_bias, ("dp", "fsdp"), axis=0, tiled=True),
        lax.all_gather(output_weight, ("dp", "fsdp"), axis=0, tiled=True),
        lax.all_gather(output_bias, ("dp", "fsdp"), axis=0, tiled=True),
        lax.all_gather(first_gain, ("dp", "fsdp"), axis=0, tiled=True),
        lax.all_gather(first_shift, ("dp", "fsdp"), axis=0, tiled=True),
        lax.all_gather(inner_weight, ("dp", "fsdp"), axis=0, tiled=True),
        lax.all_gather(inner_bias, ("dp", "fsdp"), axis=0, tiled=True),
        lax.all_gather(outer_weight, ("dp", "fsdp"), axis=0, tiled=True),
        lax.all_gather(outer_bias, ("dp", "fsdp"), axis=0, tiled=True),
        lax.all_gather(second_gain, ("dp", "fsdp"), axis=0, tiled=True),
        lax.all_gather(second_shift, ("dp", "fsdp"), axis=0, tiled=True),
    )
    (
        query_mat,
        query_vec,
        key_mat,
        value_mat,
        value_vec,
        output_mat,
        output_vec,
        first_scale,
        first_offset,
        inner_mat,
        inner_vec,
        outer_mat,
        outer_vec,
        second_scale,
        second_offset,
    ) = gathered
    query_rows = (matmul(frames, query_mat) + query_vec.astype(jnp.float32)).astype(jnp.bfloat16)
    key_rows = matmul(frames, key_mat).astype(jnp.bfloat16)
    value_rows = (matmul(frames, value_mat) + value_vec.astype(jnp.float32)).astype(jnp.bfloat16)
    query_heads = query_rows.reshape(frame_count, HEADS, head_size)
    key_heads = key_rows.reshape(frame_count, HEADS, head_size)
    value_heads = value_rows.reshape(frame_count, HEADS, head_size)
    scores = block_scores(query_heads, key_heads, groups, groups, score_scale)
    row_max = jnp.max(scores, axis=-1, keepdims=True)
    raw_weights = jnp.exp(scores - row_max)
    row_total = jnp.sum(raw_weights, axis=-1, keepdims=True)
    attn_prob = raw_weights / row_total
    log_totals = row_max + jnp.log(row_total)
    context_parts = jnp.einsum(
        "hqk,khd->qhd",
        attn_prob.astype(jnp.bfloat16),
        value_heads,
        preferred_element_type=jnp.float32,
    )
    context_rows = context_parts.reshape(frame_count, model_width).astype(jnp.bfloat16)
    frames_float = frames.astype(jnp.float32)
    resid_one = frames_float + matmul(context_rows, output_mat) + output_vec.astype(jnp.float32)
    hidden, first_pull = jax.vjp(
        layer_norm, resid_one, first_scale.astype(jnp.float32), first_offset.astype(jnp.float32)
    )
    hidden_low = hidden.astype(jnp.bfloat16)
    inner_pre = matmul(hidden_low, inner_mat) + inner_vec.astype(jnp.float32)
    active, gelu_pull = jax.vjp(exact_gelu, inner_pre)
    active_low = active.astype(jnp.bfloat16)
    outer_out = matmul(active_low, outer_mat) + outer_vec.astype(jnp.float32)
    normed_out, second_pull = jax.vjp(
        layer_norm,
        hidden + outer_out,
        second_scale.astype(jnp.float32),
        second_offset.astype(jnp.float32),
    )
    layer_out = (normed_out * live_mask[:, None]).astype(jnp.bfloat16)
    grad_top = grad_out.astype(jnp.float32) * live_mask[:, None]
    grad_two, second_gain_grad, second_shift_grad = second_pull(grad_top)
    grad_outer = grad_two.astype(jnp.bfloat16)
    outer_mat_grad = matmul_tn(active_low, grad_outer)
    outer_vec_grad = column_sums(grad_outer)
    (grad_inner,) = gelu_pull(matmul_nt(grad_outer, outer_mat))
    grad_inner_low = grad_inner.astype(jnp.bfloat16)
    inner_mat_grad = matmul_tn(hidden_low, grad_inner_low)
    inner_vec_grad = column_sums(grad_inner_low)
    grad_hidden = grad_two + matmul_nt(grad_inner_low, inner_mat)
    grad_one, first_gain_grad, first_shift_grad = first_pull(grad_hidden)
    grad_attn = grad_one.astype(jnp.bfloat16)
    output_mat_grad = matmul_tn(context_rows, grad_attn)
    output_vec_grad = column_sums(grad_attn)
    grad_context = (
        matmul_nt(grad_attn, output_mat).astype(jnp.bfloat16).reshape(frame_count, HEADS, head_size)
    )
    scores = block_scores(query_heads, key_heads, groups, groups, score_scale)
    attn_prob = jnp.exp(scores - log_totals)
    grad_prob = jnp.einsum(
        "qhd,khd->hqk", grad_context, value_heads, preferred_element_type=jnp.float32
    )
    inner_sum = jnp.sum(attn_prob * grad_prob, axis=-1, keepdims=True)
    grad_scores = (attn_prob * (grad_prob - inner_sum)).astype(jnp.bfloat16)
    query_grad_parts = (
        jnp.einsum("hqk,khd->qhd", grad_scores, key_heads, preferred_element_type=jnp.float32)
        * score_scale
    )
    key_grad_sum = (
        jnp.einsum("hqk,qhd->khd", grad_scores, query_heads, preferred_element_type=jnp.float32)
        * score_scale
    )
    value_grad_sum = jnp.einsum(
        "hqk,qhd->khd",
        attn_prob.astype(jnp.bfloat16),
        grad_context,
        preferred_element_type=jnp.float32,
    )
    grad_query = query_grad_parts.reshape(frame_count, model_width).astype(jnp.bfloat16)
    grad_key = key_grad_sum.reshape(frame_count, model_width).astype(jnp.bfloat16)
    grad_value = value_grad_sum.reshape(frame_count, model_width).astype(jnp.bfloat16)
    query_mat_grad = matmul_tn(frames, grad_query)
    query_vec_grad = column_sums(grad_query)
    key_mat_grad = matmul_tn(frames, grad_key)
    value_mat_grad = matmul_tn(frames, grad_value)
    value_vec_grad = column_sums(grad_value)
    frames_grad = (
        grad_one
        + matmul_nt(grad_query, query_mat)
        + matmul_nt(grad_key, key_mat)
        + matmul_nt(grad_value, value_mat)
    ).astype(jnp.bfloat16)
    shares = (
        lax.psum_scatter(query_mat_grad, ("dp", "fsdp"), scatter_dimension=0, tiled=True),
        lax.psum_scatter(query_vec_grad, ("dp", "fsdp"), scatter_dimension=0, tiled=True),
        lax.psum_scatter(key_mat_grad, ("dp", "fsdp"), scatter_dimension=0, tiled=True),
        lax.psum_scatter(value_mat_grad, ("dp", "fsdp"), scatter_dimension=0, tiled=True),
        lax.psum_scatter(value_vec_grad, ("dp", "fsdp"), scatter_dimension=0, tiled=True),
        lax.psum_scatter(output_mat_grad, ("dp", "fsdp"), scatter_dimension=0, tiled=True),
        lax.psum_scatter(output_vec_grad, ("dp", "fsdp"), scatter_dimension=0, tiled=True),
        lax.psum_scatter(first_gain_grad, ("dp", "fsdp"), scatter_dimension=0, tiled=True),
        lax.psum_scatter(first_shift_grad, ("dp", "fsdp"), scatter_dimension=0, tiled=True),
        lax.psum_scatter(inner_mat_grad, ("dp", "fsdp"), scatter_dimension=0, tiled=True),
        lax.psum_scatter(inner_vec_grad, ("dp", "fsdp"), scatter_dimension=0, tiled=True),
        lax.psum_scatter(outer_mat_grad, ("dp", "fsdp"), scatter_dimension=0, tiled=True),
        lax.psum_scatter(outer_vec_grad, ("dp", "fsdp"), scatter_dimension=0, tiled=True),
        lax.psum_scatter(second_gain_grad, ("dp", "fsdp"), scatter_dimension=0, tiled=True),
        lax.psum_scatter(second_shift_grad, ("dp", "fsdp"), scatter_dimension=0, tiled=True),
    )
    return (
        layer_out,
        frames_grad,
        shares[0],
        shares[1],
        shares[2],
        shares[3],
        shares[4],
        shares[5],
        shares[6],
        shares[7],
        shares[8],
        shares[9],
        shares[10],
        shares[11],
        shares[12],
        shares[13],
        shares[14],
    )


def solution(mesh):
    in_specs = (
        P(("dp", "fsdp"), None),
        P(("dp", "fsdp"), None),
        P(("dp", "fsdp"), None),
        P(("dp", "fsdp")),
        P(("dp", "fsdp"), None),
        P(("dp", "fsdp"), None),
        P(("dp", "fsdp")),
        P(("dp", "fsdp"), None),
        P(("dp", "fsdp")),
        P(("dp", "fsdp")),
        P(("dp", "fsdp")),
        P(("dp", "fsdp"), None),
        P(("dp", "fsdp")),
        P(("dp", "fsdp"), None),
        P(("dp", "fsdp")),
        P(("dp", "fsdp")),
        P(("dp", "fsdp")),
        P(("dp", "fsdp"), None),
    )
    out_specs = (
        P(("dp", "fsdp"), None),
        P(("dp", "fsdp"), None),
        P(("dp", "fsdp"), None),
        P(("dp", "fsdp")),
        P(("dp", "fsdp"), None),
        P(("dp", "fsdp"), None),
        P(("dp", "fsdp")),
        P(("dp", "fsdp"), None),
        P(("dp", "fsdp")),
        P(("dp", "fsdp")),
        P(("dp", "fsdp")),
        P(("dp", "fsdp"), None),
        P(("dp", "fsdp")),
        P(("dp", "fsdp"), None),
        P(("dp", "fsdp")),
        P(("dp", "fsdp")),
        P(("dp", "fsdp")),
    )
    return jax.shard_map(
        per_device, mesh=mesh, in_specs=in_specs, out_specs=out_specs, check_vma=False
    )
```

profile of v0, /device:TPU:0, one launch (start us, length us, event | category | flops | bytes accessed | tf_op | source)
XLA Modules:
  0.0 1126.1 jit_solution(13629870146439847360)
XLA Ops:
  11.2 0.8 dynamic-update-slice
  12.1 0.8 dynamic-update-slice.1
  12.9 0.8 dynamic-update-slice.2
  13.7 0.8 dynamic-update-slice.4
  14.6 0.8 dynamic-update-slice.3
  15.4 0.8 dynamic-update-slice.6
  16.2 0.8 dynamic-update-slice.8
  17.1 0.8 dynamic-update-slice.7
  17.9 0.8 dynamic-update-slice.5
  18.8 42.6 %all-reduce.19 = (bf16[768]{0:T(1024)(128)(2,1)S(1)}, bf16[768]{0:T(1024)(128)(2,1)S(1)}, bf16[768]{0:T(1024)(128)(2,1)S(1)}, bf16[768]{0:T(1024)(128)(2,1)S(1)}...) all-reduce(bf16[768]{0:T(1024)(128)(2,1)S(1)} %dynamic-update-slice, ...), channel_id=1, replica_groups=mesh['dp'=4,'fsdp'=8] {'dp','fsdp'}, use_global_device_ids=true, to_apply=%add | all-reduce | flops 9216 | bytes 36864
  61.4 1.3 fusion.35
  65.1 3.0 all-gather.7.cloned.1.call-done
  68.1 2.3 add_convert_fusion.3
  70.4 54.0 %all-gather.9.cloned.1.call-done = bf16[768,768]{1,0:T(8,128)(2,1)} async-done(((bf16[24,768]{1,0:T(8,128)(2,1)}), bf16[768,768]{1,0:T(8,128)(2,1)}) %all-gather.9.cloned.1.call-update) | async-done | bytes 1179664 | tf_op jit(solution)/shard_map/all_gather | solution.py:77
  124.4 2.9 add_convert_fusion.2
  127.6 1.7 copy.73
  129.3 51.2 %all-gather.11.cloned.1.call-done = bf16[768,768]{1,0:T(8,128)(2,1)} async-done(((bf16[24,768]{1,0:T(8,128)(2,1)}), bf16[768,768]{1,0:T(8,128)(2,1)}) %all-gather.11.cloned.1.call-update) | async-done | bytes 1179664 | tf_op jit(solution)/shard_map/all_gather | solution.py:79
  180.5 2.9 convolution_convert_fusion.1
  183.4 1.4 copy.74
  184.8 2.1 fusion.12
  186.9 2.6 fusion
  189.5 2.0 copy-done
  191.5 4.4 fusion.18
  195.8 40.6 %all-gather.13.cloned.1.call-done = bf16[768,768]{1,0:T(8,128)(2,1)} async-done(((bf16[24,768]{1,0:T(8,128)(2,1)}), bf16[768,768]{1,0:T(8,128)(2,1)}) %all-gather.13.cloned.1.call-update) | async-done | bytes 1179664 | tf_op jit(solution)/shard_map/all_gather | solution.py:82
  236.5 2.4 fusion.36
  238.9 1.1 copy-done.7
  240.4 61.6 %all-gather.15.cloned.1.call-done = bf16[768,3072]{1,0:T(8,128)(2,1)} async-done(((bf16[24,3072]{1,0:T(8,128)(2,1)}), bf16[768,3072]{1,0:T(8,128)(2,1)}) %all-gather.15.cloned.1.call-update) | async-done | bytes 4718608 | tf_op jit(solution)/shard_map/all_gather | solution.py:86
  301.9 21.0 %multiply_convert_fusion.1 = (bf16[512,3072]{1,0:T(8,128)(2,1)}, f32[512,3072]{1,0:T(8,128)}, f32[512,3072]{1,0:T(8,128)}) fusion(f32[3072]{0:T(1024)S(1)} %convert_element_type.159, bf16[768,3072]{1,0:T(8,128)(2,1)} %all-gather.15.cloned.1.call-done, f32[512,768]{1,0:T(8,128)} %copy-done.7, f32[768]{0:T(1024)S(1)} %convert_element_type.157, ...), kind=kOutput, calls=%fused_computation.14 | convolution fusion | flops 2521694208 | bytes 22042624 | tf_op jit(solution)/shard_map/dot_general | solution.py:20
  322.9 44.4 %all-gather.17.cloned.1.call-done = bf16[3072,768]{1,0:T(8,128)(2,1)} async-done(((bf16[96,768]{1,0:T(8,128)(2,1)}), bf16[3072,768]{1,0:T(8,128)(2,1)}) %all-gather.17.cloned.1.call-update) | async-done | bytes 4718608 | tf_op jit(solution)/shard_map/all_gather | solution.py:88
  367.3 6.1 fusion.37
  374.6 1.7 fusion.33
  377.2 8.5 convert_reduce_fusion
  385.7 3.1 multiply_reduce_fusion.2
  389.8 0.9 copy-done.14
  390.7 1.7 convolution_convert_fusion
  392.4 2.3 copy.76
  394.7 13.5 %multiply_reduce_fusion = (f32[12,512]{1,0:T(8,128)S(1)}, f32[12,512,512]{1,2,0:T(8,128)}) fusion(f32[12,512]{1,0:T(8,128)S(1)} %log_add_fusion, f32[12,512,512]{1,2,0:T(8,128)} %copy-done, pred[512,512]{0,1:T(8,128)(4,1)S(1)} %broadcast_compare_fusion, bf16[512,12,64]{0,2,1:T(8,128)(2,1)} %bitcast.82, bf16[512,12,64]{0,2,1:T(8,128)(2,1)} %bitcast.81), kind=kOutput, calls=%fused_computation.1 | convolution fusion | flops 418375680 | bytes 27049984 | tf_op jit(solution)/shard_map/qhd,khd->hqk/dot_general | solution.py:165
  408.3 7.0 multiply_convert_fusion
  415.3 1.2 convert_reduce_fusion.4
  416.5 1.4 copy-done.1
  417.9 0.9 copy-done.5
  418.8 2.2 convolution_bitcast_fusion.2
  421.0 3.1 copy.87
  424.4 4.8 multiply_convert_fusion.2
  429.2 0.9 copy-done.17
  430.1 2.2 convolution_bitcast_fusion.1
  432.3 3.2 copy.89
  435.6 6.6 convert_reduce_fusion.3
  442.2 0.9 copy-done.15
  443.1 2.2 convolution_bitcast_fusion
  445.3 3.2 copy.91
  448.6 3.7 fusion.40
  452.3 7.3 fusion.28
  459.7 1.1 copy-done.21
  460.7 8.2 fusion.41
  469.1 40.9 %all-reduce.18 = (f32[768]{0:T(1024)S(1)}, f32[768]{0:T(1024)S(1)}, f32[768]{0:T(1024)S(1)}, f32[768]{0:T(1024)S(1)}, f32[768]{0:T(1024)S(1)}, /*index=5*/f32[30...) all-reduce(f32[768]{0:T(1024)S(1)} %reduce_sum.228, ...), channel_id=3, replica_groups=mesh['dp'=4,'fsdp'=8] {'dp','fsdp'}, use_global_device_ids=true, to_apply=%region_14.15.clone | all-reduce | flops 9216 | bytes 73728
  515.3 2.2 fusion.39
  518.5 2.0 add_convert_fusion.1
  520.4 2.0 reduce-scatter.19.cloned.1.call-done
  522.4 104.8 %reduce-scatter.21.cloned.1.call-done = f32[24,768]{1,0:T(8,128)} async-done(((f32[768,768]{1,0:T(8,128)}), f32[24,768]{1,0:T(8,128)}) %reduce-scatter.21.cloned.1.call-update) | async-done | bytes 73744
  627.2 103.9 %reduce-scatter.23.cloned.1.call-done = f32[24,768]{1,0:T(8,128)} async-done(((f32[768,768]{1,0:T(8,128)}), f32[24,768]{1,0:T(8,128)}) %reduce-scatter.23.cloned.1.call-update) | async-done | bytes 73744
  731.2 104.6 %reduce-scatter.13.cloned.1.call-done = f32[24,768]{1,0:T(8,128)} async-done(((f32[768,768]{1,0:T(8,128)}), f32[24,768]{1,0:T(8,128)}) %reduce-scatter.13.cloned.1.call-update) | async-done | bytes 73744 | tf_op jit(solution)/shard_map/reduce_scatter | solution.py:204
  835.7 141.0 %reduce-scatter.15.cloned.1.call-done = f32[24,3072]{1,0:T(8,128)} async-done(((f32[768,3072]{1,0:T(8,128)}), f32[24,3072]{1,0:T(8,128)}) %reduce-scatter.15.cloned.1.call-update) | async-done | bytes 294928 | tf_op jit(solution)/shard_map/reduce_scatter | solution.py:208
  976.8 141.9 %reduce-scatter.17.cloned.1.call-done = f32[96,768]{1,0:T(8,128)} async-done(((f32[3072,768]{1,0:T(8,128)}), f32[96,768]{1,0:T(8,128)}) %reduce-scatter.17.cloned.1.call-update) | async-done | bytes 294928 | tf_op jit(solution)/shard_map/reduce_scatter | solution.py:210
  (130 shorter events, 15.3 us)
Async XLA Ops:
  7.2 117.2 %copy-start.2 = (bf16[512,768]{1,0:T(8,128)(2,1)S(1)}, bf16[512,768]{1,0:T(8,128)(2,1)}, u32[]{:S(2)}) copy-start(bf16[512,768]{1,0:T(8,128)(2,1)} %param.18) | copy-start | bytes 2359300
  7.2 60.9 %all-gather.7.cloned.1.call-start = ((), (), s32[]{:S(2)}) async-start(), calls=%async_computation.6 | async-start | bytes 1216512 | tf_op jit(solution)/shard_map/all_gather | solution.py:80
  7.9 116.4 %all-gather.9.cloned.1.call-start = ((), (), s32[]{:S(2)}) async-start(), calls=%async_computation.7 | async-start | bytes 1216512 | tf_op jit(solution)/shard_map/all_gather | solution.py:77
  8.7 171.8 %all-gather.11.cloned.1.call-start = ((), (), s32[]{:S(2)}) async-start(), calls=%async_computation.8 | async-start | bytes 1216512 | tf_op jit(solution)/shard_map/all_gather | solution.py:79
  9.4 227.0 %all-gather.13.cloned.1.call-start = ((), (), s32[]{:S(2)}) async-start(), calls=%async_computation.9 | async-start | bytes 1216512 | tf_op jit(solution)/shard_map/all_gather | solution.py:82
  10.0 292.0 %all-gather.15.cloned.1.call-start = ((), (), s32[]{:S(2)}) async-start(), calls=%async_computation.10 | async-start | bytes 4866048 | tf_op jit(solution)/shard_map/all_gather | solution.py:86
  10.6 356.7 %all-gather.17.cloned.1.call-start = ((), (), s32[]{:S(2)}) async-start(), calls=%async_computation.11 | async-start | bytes 4866048 | tf_op jit(solution)/shard_map/all_gather | solution.py:88
  11.2 511.3 %reduce-scatter.19.cloned.1.call-start = ((), (), s32[]{:S(2)}) async-start(), calls=%async_computation.15 | async-start | bytes 2433024
  127.6 61.9 %copy-start.11 = (bf16[512,768]{0,1:T(8,128)(2,1)}, bf16[512,768]{0,1:T(8,128)(2,1)S(1)}, u32[]{:S(2)}) copy-start(bf16[512,768]{0,1:T(8,128)(2,1)S(1)} %copy.72) | copy-start | bytes 2359300
  186.9 4.6 copy-start
  238.9 1.2 copy-start.7
  240.4 126.9 %copy-start.8 = (f32[512,768]{1,0:T(8,128)S(1)}, f32[512,768]{1,0:T(8,128)}, u32[]{:S(2)}) copy-start(f32[512,768]{1,0:T(8,128)} %copy-done.7) | copy-start | bytes 4718596
  367.3 6.4 copy-start.13
  374.6 2.6 copy-start.22
  376.3 9.4 slice-start.3
  376.5 9.2 copy-start.20
  377.2 8.5 slice-start.4
  385.7 3.2 copy-start.25
  385.7 3.2 copy-start.9
  388.9 1.8 copy-start.24
  389.8 0.9 copy-start.14
  394.7 13.5 %slice-start = ((s8[12582912]{0:T(1024)(128)(4,1)}), s8[4194304]{0:T(1024)(128)(4,1)S(1)}, s32[]{:S(2)}) async-start(s8[12582912]{0:T(1024)(128)(4,1)} %bitcast.72), calls=%async_computation.18 | async-start | bytes 8388608
  394.7 13.5 %slice-start.1 = ((s8[12582912]{0:T(1024)(128)(4,1)}), s8[4194304]{0:T(1024)(128)(4,1)S(1)}, s32[]{:S(2)}) async-start(s8[12582912]{0:T(1024)(128)(4,1)} %bitcast.72), calls=%async_computation.19 | async-start | bytes 8388608
  394.7 13.5 %slice-start.2 = ((s8[12582912]{0:T(1024)(128)(4,1)}), s8[4194304]{0:T(1024)(128)(4,1)S(1)}, s32[]{:S(2)}) async-start(s8[12582912]{0:T(1024)(128)(4,1)} %bitcast.72), calls=%async_computation.20 | async-start | bytes 8388608
  415.3 2.6 copy-start.1
  415.3 3.5 copy-start.3
  417.8 0.9 copy-start.5
  424.1 6.0 copy-start.4
  424.1 203.1 %reduce-scatter.21.cloned.1.call-start = ((), (), s32[]{:S(2)}) async-start(), calls=%async_computation.16 | async-start | bytes 2433024
  429.2 0.9 copy-start.17
  432.3 3.3 copy-start.12
  435.5 295.7 %reduce-scatter.23.cloned.1.call-start = ((), (), s32[]{:S(2)}) async-start(), calls=%async_computation.17 | async-start | bytes 2433024
  442.2 0.9 copy-start.15
  448.5 3.8 copy-start.10
  448.5 387.2 %reduce-scatter.13.cloned.1.call-start = ((), (), s32[]{:S(2)}) async-start(), calls=%async_computation.12 | async-start | bytes 2433024 | tf_op jit(solution)/shard_map/reduce_scatter | solution.py:204
  452.3 524.5 %reduce-scatter.15.cloned.1.call-start = ((), (), s32[]{:S(2)}) async-start(), calls=%async_computation.13 | async-start | bytes 9732096 | tf_op jit(solution)/shard_map/reduce_scatter | solution.py:208
  459.6 1.1 copy-start.21
  459.6 659.1 %reduce-scatter.17.cloned.1.call-start = ((), (), s32[]{:S(2)}) async-start(), calls=%async_computation.14 | async-start | bytes 9732096 | tf_op jit(solution)/shard_map/reduce_scatter | solution.py:210
  468.9 46.4 %copy-start.18 = (bf16[12,64,512]{2,1,0:T(8,128)(2,1)S(1)}, bf16[12,64,512]{2,1,0:T(8,128)(2,1)}, u32[]{:S(2)}) copy-start(bf16[12,64,512]{2,1,0:T(8,128)(2,1)} %copy-done.17) | copy-start | bytes 2359300
  469.0 48.6 %copy-start.6 = (bf16[12,64,512]{2,1,0:T(8,128)(2,1)S(1)}, bf16[12,64,512]{2,1,0:T(8,128)(2,1)}, u32[]{:S(2)}) copy-start(bf16[12,64,512]{2,1,0:T(8,128)(2,1)} %copy-done.5) | copy-start | bytes 2359300
  510.1 7.5 copy-start.23
  515.3 3.1 copy-start.16
  515.3 3.1 copy-start.19
Sparse Core Ops, SparseCore 0:
  11.0 57.0 all-gather.6
  71.1 53.2 all-gather.8
  127.4 53.0 all-gather.10
  183.3 53.0 all-gather.12
  239.3 62.6 all-gather.14
  304.8 62.4 all-gather.16
  424.2 98.1 reduce-scatter.18
  529.1 98.0 reduce-scatter.20
  633.1 98.0 reduce-scatter.22
  737.7 97.9 reduce-scatter.12
  842.2 134.5 reduce-scatter.14
  984.1 134.5 reduce-scatter.16
where the time goes:
time: 1140 us; the launch traced here: 1130 us
  waiting for transfers between devices  857 us (75%)
  matrix products  114 us (10%)
  blocking collectives  83.5 us (7%)
  local copies, waits for them, and re-layouts  39.3 us (3%)
  between operations  16.5 us (1%)
  other arithmetic  14.8 us (1%)
    unnamed x15, waiting for transfers between devices  214 us
    reduce_scatter x1, waiting for transfers between devices, per_device(): lax.psum_scatter(outer_mat_grad, ('dp', 'fsdp'), scatter_dimension=0, til...  142 us
    reduce_scatter x1, waiting for transfers between devices, per_device(): lax.psum_scatter(inner_mat_grad, ('dp', 'fsdp'), scatter_dimension=0, til...  141 us
    reduce_scatter x1, waiting for transfers between devices, per_device(): lax.psum_scatter(output_mat_grad, ('dp', 'fsdp'), scatter_dimension=0, ti...  105 us
    unnamed x2, blocking collectives  83.5 us
    all_gather x1, waiting for transfers between devices, per_device(): lax.all_gather(inner_weight, ('dp', 'fsdp'), axis=0, tiled=True)  61.6 us
    all_gather x1, waiting for transfers between devices, per_device(): lax.all_gather(query_weight, ('dp', 'fsdp'), axis=0, tiled=True)  54 us
    all_gather x1, waiting for transfers between devices, per_device(): lax.all_gather(key_weight, ('dp', 'fsdp'), axis=0, tiled=True)  51.2 us
  transfers between devices with their start and end apart: 12, of which 12 were waited for; matrix products, arithmetic and copies ran while one was open for 9% of the time, Pallas kernels for 0%

commit v1 on v0

--- a/solution.py
+++ b/solution.py
@@ -4,6 +4,28 @@
 from jax.sharding import PartitionSpec as P
 
 HEADS = 12
+
+
+def laid_out(tiles, dim):
+    lengths = list(tiles.shape[1:])
+    lengths[dim] *= tiles.shape[0]
+    return jnp.moveaxis(tiles, 0, dim).reshape(lengths)
+
+
+def grow_blocks(x, axis):
+    length = lax.axis_size(axis)
+    parts = x[None]
+    for level in range(length.bit_length() - 1):
+        bit = 1 << level
+        other = lax.ppermute(parts, axis, [(i, i ^ bit) for i in range(length)])
+        both = jnp.stack([parts, other])
+        upper = lax.axis_index(axis) >> level & 1
+        parts = jnp.where(upper == 0, both, both[::-1]).reshape(-1, *x.shape)
+    return parts
+
+
+def doubled_up(x, axis, dim):
+    return laid_out(grow_blocks(x, axis), dim)
 
 
 def layer_norm(values, gain_vec, shift_vec):
@@ -79,7 +101,7 @@
         lax.all_gather(key_weight, ("dp", "fsdp"), axis=0, tiled=True),
         lax.all_gather(value_weight, ("dp", "fsdp"), axis=0, tiled=True),
         lax.all_gather(value_bias, ("dp", "fsdp"), axis=0, tiled=True),
-        lax.all_gather(output_weight, ("dp", "fsdp"), axis=0, tiled=True),
+        doubled_up(output_weight, ("dp", "fsdp"), 0),
         lax.all_gather(output_bias, ("dp", "fsdp"), axis=0, tiled=True),
         lax.all_gather(first_gain, ("dp", "fsdp"), axis=0, tiled=True),
         lax.all_gather(first_shift, ("dp", "fsdp"), axis=0, tiled=True),

time: 1140 us -> 1080 us (0.947)
  waiting for transfers between devices: 857 us -> 795 us
    all_gather x1 -> x0, waiting for transfers between devices: 40.6 us -> none  [per_device(): lax.all_gather(output_weight, ('dp', 'fsdp'), axis=0, tiled=True)]
    all_gather x1, waiting for transfers between devices: 54 us -> 38.2 us  [per_device(): lax.all_gather(query_weight, ('dp', 'fsdp'), axis=0, tiled=True)]
    all_gather x1, waiting for transfers between devices: 61.6 us -> 48.5 us  [per_device(): lax.all_gather(inner_weight, ('dp', 'fsdp'), axis=0, tiled=True)]
    unnamed x92 -> x116, local copies, waits for them, and re-layouts: 32.1 us -> 26.6 us
    unnamed x15 -> x14, waiting for transfers between devices: 214 us -> 214 us
  transfers between devices with their start and end apart: 12 -> 16, of which waited for: 12 -> 14; matrix products, arithmetic and copies ran while one was open for 9% -> 9% of each run, Pallas kernels for 0% -> 0%
where the time goes in v1:
time: 1080 us; the launch traced here: 1070 us
  waiting for transfers between devices  795 us (74%)
  matrix products  112 us (10%)
  blocking collectives  87.2 us (8%)
  local copies, waits for them, and re-layouts  33.1 us (3%)
  other arithmetic  17.3 us (2%)
  between operations  16.1 us (1%)
  starting transfers between devices  10.9 us (1%)
    unnamed x14, waiting for transfers between devices  214 us
    reduce_scatter x1, waiting for transfers between devices, per_device(): lax.psum_scatter(outer_mat_grad, ('dp', 'fsdp'), scatter_dimension=0, til...  142 us
    reduce_scatter x1, waiting for transfers between devices, per_device(): lax.psum_scatter(inner_mat_grad, ('dp', 'fsdp'), scatter_dimension=0, til...  141 us
    reduce_scatter x1, waiting for transfers between devices, per_device(): lax.psum_scatter(output_mat_grad, ('dp', 'fsdp'), scatter_dimension=0, ti...  105 us
    unnamed x2, blocking collectives  87.2 us
    all_gather x1, waiting for transfers between devices, per_device(): lax.all_gather(key_weight, ('dp', 'fsdp'), axis=0, tiled=True)  51.2 us
    all_gather x1, waiting for transfers between devices, per_device(): lax.all_gather(inner_weight, ('dp', 'fsdp'), axis=0, tiled=True)  48.5 us
    all_gather x1, waiting for transfers between devices, per_device(): lax.all_gather(outer_weight, ('dp', 'fsdp'), axis=0, tiled=True)  44.3 us
  transfers between devices with their start and end apart: 16, of which 14 were waited for; matrix products, arithmetic and copies ran while one was open for 9% of the time, Pallas kernels for 0%

profile of v1, /device:TPU:0, one launch (start us, length us, event | category | flops | bytes accessed | tf_op | source)
XLA Modules:
  0.0 1071.4 jit_solution(13943416034005737071)
XLA Ops:
  10.1 3.0 collective-permute-start
  13.1 2.1 collective-permute-done
  15.3 0.8 pad_maximum_fusion.4
  16.1 2.2 collective-permute-start.1
  18.3 2.3 collective-permute-done.1
  20.6 3.1 collective-permute-start.2
  23.7 5.0 collective-permute-done.2
  29.0 1.5 collective-permute-done.3
  30.6 1.9 collective-permute-start.4
  35.3 46.4 %all-reduce.19 = (bf16[768]{0:T(1024)(128)(2,1)S(1)}, bf16[768]{0:T(1024)(128)(2,1)S(1)}, bf16[768]{0:T(1024)(128)(2,1)S(1)}, bf16[768]{0:T(1024)(128)(2,1)S(1)}...) all-reduce(bf16[768]{0:T(1024)(128)(2,1)S(1)} %dynamic-update-slice, ...), channel_id=1, replica_groups=mesh['dp'=4,'fsdp'=8] {'dp','fsdp'}, use_global_device_ids=true, to_apply=%add | all-reduce | flops 9216 | bytes 36864
  84.2 1.3 reverse_select_fusion
  85.5 2.1 add_convert_fusion.3
  87.6 38.2 %all-gather.8.cloned.1.call-done = bf16[768,768]{1,0:T(8,128)(2,1)} async-done(((bf16[24,768]{1,0:T(8,128)(2,1)}), bf16[768,768]{1,0:T(8,128)(2,1)}) %all-gather.8.cloned.1.call-update) | async-done | bytes 1179664 | tf_op jit(solution)/shard_map/all_gather | solution.py:99
  125.8 2.9 add_convert_fusion.2
  129.0 1.7 copy.73
  130.7 51.2 %all-gather.10.cloned.1.call-done = bf16[768,768]{1,0:T(8,128)(2,1)} async-done(((bf16[24,768]{1,0:T(8,128)(2,1)}), bf16[768,768]{1,0:T(8,128)(2,1)}) %all-gather.10.cloned.1.call-update) | async-done | bytes 1179664 | tf_op jit(solution)/shard_map/all_gather | solution.py:101
  181.9 2.9 convolution_convert_fusion.1
  184.8 1.4 copy.74
  186.2 2.1 fusion.12
  188.3 2.6 fusion
  190.9 1.9 copy-done
  192.8 3.6 fusion.18
  196.4 0.9 fusion.38
  197.4 1.1 copy-done.7
  198.8 48.5 %all-gather.12.cloned.1.call-done = bf16[768,3072]{1,0:T(8,128)(2,1)} async-done(((bf16[24,3072]{1,0:T(8,128)(2,1)}), bf16[768,3072]{1,0:T(8,128)(2,1)}) %all-gather.12.cloned.1.call-update) | async-done | bytes 4718608 | tf_op jit(solution)/shard_map/all_gather | solution.py:108
  247.4 21.0 %multiply_convert_fusion.1 = (bf16[512,3072]{1,0:T(8,128)(2,1)}, f32[512,3072]{1,0:T(8,128)}, f32[512,3072]{1,0:T(8,128)}) fusion(f32[3072]{0:T(1024)S(1)} %convert_element_type.161, bf16[768,3072]{1,0:T(8,128)(2,1)} %all-gather.12.cloned.1.call-done, f32[512,768]{1,0:T(8,128)} %copy-done.7, f32[768]{0:T(1024)S(1)} %convert_element_type.159, ...), kind=kOutput, calls=%fused_computation.14 | convolution fusion | flops 2521694208 | bytes 22042624 | tf_op jit(solution)/shard_map/dot_general | solution.py:42
  268.4 44.3 %all-gather.14.cloned.1.call-done = bf16[3072,768]{1,0:T(8,128)(2,1)} async-done(((bf16[96,768]{1,0:T(8,128)(2,1)}), bf16[3072,768]{1,0:T(8,128)(2,1)}) %all-gather.14.cloned.1.call-update) | async-done | bytes 4718608 | tf_op jit(solution)/shard_map/all_gather | solution.py:110
  312.7 6.1 fusion.39
  319.2 0.8 multiply_reduce_fusion.1
  320.0 1.7 fusion.35
  322.6 8.7 convert_reduce_fusion
  331.3 3.2 multiply_reduce_fusion.2
  335.4 0.9 copy-done.14
  336.3 1.7 convolution_convert_fusion
  338.0 2.3 copy.76
  340.3 13.5 %multiply_reduce_fusion = (f32[12,512]{1,0:T(8,128)S(1)}, f32[12,512,512]{1,2,0:T(8,128)}) fusion(f32[12,512]{1,0:T(8,128)S(1)} %log_add_fusion, f32[12,512,512]{1,2,0:T(8,128)} %copy-done, pred[512,512]{0,1:T(8,128)(4,1)S(1)} %broadcast_compare_fusion, bf16[512,12,64]{0,2,1:T(8,128)(2,1)} %bitcast.100, bf16[512,12,64]{0,2,1:T(8,128)(2,1)} %bitcast.99), kind=kOutput, calls=%fused_computation.1 | convolution fusion | flops 418375680 | bytes 27049984 | tf_op jit(solution)/shard_map/qhd,khd->hqk/dot_general | solution.py:187
  353.9 7.0 multiply_convert_fusion
  360.9 1.2 convert_reduce_fusion.4
  362.1 1.4 copy-done.1
  363.5 0.9 copy-done.5
  364.4 2.2 convolution_bitcast_fusion.2
  366.6 3.0 copy.87
  369.9 4.8 multiply_convert_fusion.2
  374.8 0.9 copy-done.17
  375.6 2.2 convolution_bitcast_fusion.1
  377.8 3.2 copy.89
  381.0 6.6 convert_reduce_fusion.3
  387.7 0.9 copy-done.15
  388.6 2.2 convolution_bitcast_fusion
  390.8 3.1 copy.91
  394.0 3.7 fusion.42
  397.8 7.3 fusion.30
  405.1 1.1 copy-done.23
  406.2 8.2 fusion.43
  414.6 40.8 %all-reduce.18 = (f32[768]{0:T(1024)S(1)}, f32[768]{0:T(1024)S(1)}, f32[768]{0:T(1024)S(1)}, f32[768]{0:T(1024)S(1)}, f32[768]{0:T(1024)S(1)}, /*index=5*/f32[30...) all-reduce(f32[768]{0:T(1024)S(1)} %reduce_sum.228, ...), channel_id=3, replica_groups=mesh['dp'=4,'fsdp'=8] {'dp','fsdp'}, use_global_device_ids=true, to_apply=%region_14.15.clone | all-reduce | flops 9216 | bytes 73728
  460.6 2.2 fusion.41
  462.9 0.8 fusion.40
  463.8 2.0 add_convert_fusion.1
  465.7 2.4 reduce-scatter.19.cloned.1.call-done
  468.1 104.8 %reduce-scatter.21.cloned.1.call-done = f32[24,768]{1,0:T(8,128)} async-done(((f32[768,768]{1,0:T(8,128)}), f32[24,768]{1,0:T(8,128)}) %reduce-scatter.21.cloned.1.call-update) | async-done | bytes 73744
  572.9 103.9 %reduce-scatter.23.cloned.1.call-done = f32[24,768]{1,0:T(8,128)} async-done(((f32[768,768]{1,0:T(8,128)}), f32[24,768]{1,0:T(8,128)}) %reduce-scatter.23.cloned.1.call-update) | async-done | bytes 73744
  676.8 104.8 %reduce-scatter.13.cloned.1.call-done = f32[24,768]{1,0:T(8,128)} async-done(((f32[768,768]{1,0:T(8,128)}), f32[24,768]{1,0:T(8,128)}) %reduce-scatter.13.cloned.1.call-update) | async-done | bytes 73744 | tf_op jit(solution)/shard_map/reduce_scatter | solution.py:226
  781.6 140.8 %reduce-scatter.15.cloned.1.call-done = f32[24,3072]{1,0:T(8,128)} async-done(((f32[768,3072]{1,0:T(8,128)}), f32[24,3072]{1,0:T(8,128)}) %reduce-scatter.15.cloned.1.call-update) | async-done | bytes 294928 | tf_op jit(solution)/shard_map/reduce_scatter | solution.py:230
  922.5 142.2 %reduce-scatter.17.cloned.1.call-done = f32[96,768]{1,0:T(8,128)} async-done(((f32[3072,768]{1,0:T(8,128)}), f32[96,768]{1,0:T(8,128)}) %reduce-scatter.17.cloned.1.call-update) | async-done | bytes 294928 | tf_op jit(solution)/shard_map/reduce_scatter | solution.py:232
  (171 shorter events, 15.7 us)
Async XLA Ops:
  7.2 25.4 %copy-start.25 = (s32[1,2]{1,0:T(1,128)S(1)}, s32[1,2]{1,0:T(1,128)}, u32[]{:S(2)}) copy-start(s32[1,2]{1,0:T(1,128)} %param.19) | copy-start | bytes 28
  7.2 26.0 %copy-start.28 = (bf16[24]{0:T(256)(128)(2,1)S(1)}, bf16[24]{0:T(256)(128)(2,1)}, u32[]{:S(2)}) copy-start(bf16[24]{0:T(256)(128)(2,1)} %param.24) | copy-start | bytes 148
  7.2 26.2 %copy-start.29 = (bf16[24]{0:T(256)(128)(2,1)S(1)}, bf16[24]{0:T(256)(128)(2,1)}, u32[]{:S(2)}) copy-start(bf16[24]{0:T(256)(128)(2,1)} %param.21) | copy-start | bytes 148
  7.2 26.4 %copy-start.30 = (bf16[24]{0:T(256)(128)(2,1)S(1)}, bf16[24]{0:T(256)(128)(2,1)}, u32[]{:S(2)}) copy-start(bf16[24]{0:T(256)(128)(2,1)} %param.26) | copy-start | bytes 148
  7.2 26.6 %copy-start.31 = (bf16[24]{0:T(256)(128)(2,1)S(1)}, bf16[24]{0:T(256)(128)(2,1)}, u32[]{:S(2)}) copy-start(bf16[24]{0:T(256)(128)(2,1)} %param.28) | copy-start | bytes 148
  7.2 26.9 %copy-start.32 = (bf16[24]{0:T(256)(128)(2,1)S(1)}, bf16[24]{0:T(256)(128)(2,1)}, u32[]{:S(2)}) copy-start(bf16[24]{0:T(256)(128)(2,1)} %param.27) | copy-start | bytes 148
  7.2 27.1 %copy-start.33 = (bf16[24]{0:T(256)(128)(2,1)S(1)}, bf16[24]{0:T(256)(128)(2,1)}, u32[]{:S(2)}) copy-start(bf16[24]{0:T(256)(128)(2,1)} %param.32) | copy-start | bytes 148
  7.3 27.3 %copy-start.34 = (bf16[24]{0:T(256)(128)(2,1)S(1)}, bf16[24]{0:T(256)(128)(2,1)}, u32[]{:S(2)}) copy-start(bf16[24]{0:T(256)(128)(2,1)} %param.34) | copy-start | bytes 148
  7.3 27.5 %copy-start.35 = (bf16[24]{0:T(256)(128)(2,1)S(1)}, bf16[24]{0:T(256)(128)(2,1)}, u32[]{:S(2)}) copy-start(bf16[24]{0:T(256)(128)(2,1)} %param.33) | copy-start | bytes 148
  7.3 27.8 %copy-start.36 = (bf16[96]{0:T(256)(128)(2,1)S(1)}, bf16[96]{0:T(256)(128)(2,1)}, u32[]{:S(2)}) copy-start(bf16[96]{0:T(256)(128)(2,1)} %param.30) | copy-start | bytes 580
  7.3 78.2 %all-gather.6.cloned.1.call-start = ((), (), s32[]{:S(2)}) async-start(), calls=%async_computation.6 | async-start | bytes 1216512 | tf_op jit(solution)/shard_map/all_gather | solution.py:102
  8.0 117.7 %all-gather.8.cloned.1.call-start = ((), (), s32[]{:S(2)}) async-start(), calls=%async_computation.7 | async-start | bytes 1216512 | tf_op jit(solution)/shard_map/all_gather | solution.py:99
  8.8 173.1 %all-gather.10.cloned.1.call-start = ((), (), s32[]{:S(2)}) async-start(), calls=%async_computation.8 | async-start | bytes 1216512 | tf_op jit(solution)/shard_map/all_gather | solution.py:101
  9.5 237.9 %all-gather.12.cloned.1.call-start = ((), (), s32[]{:S(2)}) async-start(), calls=%async_computation.9 | async-start | bytes 4866048 | tf_op jit(solution)/shard_map/all_gather | solution.py:108
  10.1 302.6 %all-gather.14.cloned.1.call-start = ((), (), s32[]{:S(2)}) async-start(), calls=%async_computation.10 | async-start | bytes 4866048 | tf_op jit(solution)/shard_map/all_gather | solution.py:110
  10.1 5.2 collective-permute-start
  16.1 4.5 collective-permute-start.1
  20.6 8.1 collective-permute-start.2
  28.8 1.6 collective-permute-start.3
  28.9 439.2 %reduce-scatter.19.cloned.1.call-start = ((), (), s32[]{:S(2)}) async-start(), calls=%async_computation.14 | async-start | bytes 2433024
  30.5 55.0 %copy-start.2 = (bf16[512,768]{1,0:T(8,128)(2,1)S(1)}, bf16[512,768]{1,0:T(8,128)(2,1)}, u32[]{:S(2)}) copy-start(bf16[512,768]{1,0:T(8,128)(2,1)} %param.18) | copy-start | bytes 2359300
  30.6 53.5 %collective-permute-start.4 = (bf16[16,24,768]{2,1,0:T(8,128)(2,1)S(1)}, bf16[16,24,768]{2,1,0:T(8,128)(2,1)S(1)}, u32[]{:S(2)}, u32[]{:S(2)}) collective-permute-start(bf16[16,24,768]{2,1,0:T(8,128)(2,1)S(1)} %bitcast.106), channel_id=1, source_target_pairs={{0,16},{1,17},{2,18},{3,19},{4,20},{5,21},{6,22},{7,23},{8,24},{9,... | collective-permute-start | bytes 1769480 | tf_op jit(solution)/shard_map/ppermute | solution.py:20
  129.0 61.9 %copy-start.11 = (bf16[512,768]{0,1:T(8,128)(2,1)}, bf16[512,768]{0,1:T(8,128)(2,1)S(1)}, u32[]{:S(2)}) copy-start(bf16[512,768]{0,1:T(8,128)(2,1)S(1)} %copy.72) | copy-start | bytes 2359300
  188.3 4.5 copy-start
  192.8 3.6 copy-start.19
  196.4 2.4 copy-start.24
  197.4 1.1 copy-start.7
  198.8 113.9 %copy-start.8 = (f32[512,768]{1,0:T(8,128)S(1)}, f32[512,768]{1,0:T(8,128)}, u32[]{:S(2)}) copy-start(f32[512,768]{1,0:T(8,128)} %copy-done.7) | copy-start | bytes 4718596
  312.7 6.4 copy-start.13
  320.0 2.6 copy-start.26
  321.7 9.6 slice-start.3
  321.9 9.4 copy-start.22
  322.6 8.7 slice-start.4
  331.3 3.2 copy-start.37
  331.3 3.2 copy-start.9
  334.5 1.8 copy-start.20
  335.4 0.9 copy-start.14
  340.3 13.5 %slice-start = ((s8[12582912]{0:T(1024)(128)(4,1)}), s8[4194304]{0:T(1024)(128)(4,1)S(1)}, s32[]{:S(2)}) async-start(s8[12582912]{0:T(1024)(128)(4,1)} %bitcast.90), calls=%async_computation.17 | async-start | bytes 8388608
  340.3 13.5 %slice-start.1 = ((s8[12582912]{0:T(1024)(128)(4,1)}), s8[4194304]{0:T(1024)(128)(4,1)S(1)}, s32[]{:S(2)}) async-start(s8[12582912]{0:T(1024)(128)(4,1)} %bitcast.90), calls=%async_computation.18 | async-start | bytes 8388608
  340.3 13.5 %slice-start.2 = ((s8[12582912]{0:T(1024)(128)(4,1)}), s8[4194304]{0:T(1024)(128)(4,1)S(1)}, s32[]{:S(2)}) async-start(s8[12582912]{0:T(1024)(128)(4,1)} %bitcast.90), calls=%async_computation.19 | async-start | bytes 8388608
  360.9 2.6 copy-start.1
  360.9 3.5 copy-start.3
  363.5 0.9 copy-start.5
  369.7 5.9 copy-start.4
  369.7 203.2 %reduce-scatter.21.cloned.1.call-start = ((), (), s32[]{:S(2)}) async-start(), calls=%async_computation.15 | async-start | bytes 2433024
  374.7 0.9 copy-start.17
  377.8 3.2 copy-start.12
  381.0 295.8 %reduce-scatter.23.cloned.1.call-start = ((), (), s32[]{:S(2)}) async-start(), calls=%async_computation.16 | async-start | bytes 2433024
  387.7 0.9 copy-start.15
  394.0 3.8 copy-start.10
  394.0 387.6 %reduce-scatter.13.cloned.1.call-start = ((), (), s32[]{:S(2)}) async-start(), calls=%async_computation.11 | async-start | bytes 2433024 | tf_op jit(solution)/shard_map/reduce_scatter | solution.py:226
  397.7 524.7 %reduce-scatter.15.cloned.1.call-start = ((), (), s32[]{:S(2)}) async-start(), calls=%async_computation.12 | async-start | bytes 9732096 | tf_op jit(solution)/shard_map/reduce_scatter | solution.py:230
  405.0 1.1 copy-start.23
  405.1 659.6 %reduce-scatter.17.cloned.1.call-start = ((), (), s32[]{:S(2)}) async-start(), calls=%async_computation.13 | async-start | bytes 9732096 | tf_op jit(solution)/shard_map/reduce_scatter | solution.py:232
  414.4 46.2 %copy-start.18 = (bf16[12,64,512]{2,1,0:T(8,128)(2,1)S(1)}, bf16[12,64,512]{2,1,0:T(8,128)(2,1)}, u32[]{:S(2)}) copy-start(bf16[12,64,512]{2,1,0:T(8,128)(2,1)} %copy-done.17) | copy-start | bytes 2359300
  414.4 48.5 %copy-start.6 = (bf16[12,64,512]{2,1,0:T(8,128)(2,1)S(1)}, bf16[12,64,512]{2,1,0:T(8,128)(2,1)}, u32[]{:S(2)}) copy-start(bf16[12,64,512]{2,1,0:T(8,128)(2,1)} %copy-done.5) | copy-start | bytes 2359300
  455.4 7.5 copy-start.27
  460.6 3.1 copy-start.16
  460.6 3.1 copy-start.21
Sparse Core Ops, SparseCore 0:
  11.1 58.5 all-gather.5
  72.6 53.0 all-gather.7
  128.8 53.0 all-gather.9
  184.7 62.6 all-gather.11
  250.2 62.4 all-gather.13
  369.8 98.2 reduce-scatter.18
  474.8 98.0 reduce-scatter.20
  578.8 97.9 reduce-scatter.22
  683.5 98.0 reduce-scatter.12
  787.9 134.4 reduce-scatter.14
  929.9 134.6 reduce-scatter.16
